TPU v7x, 512 devices: a whole 4x8x8 slice. The times are simulated.
512 devices in a mesh: dp: 64 (over y, z_lo, core), ctx: 8 (over x, z_hi).
Axes of the slice: x: 4, y: 8, z: 8 (z_hi: 2, z_lo: 4; z = z_hi * 4 + z_lo), core: 2. Of those that a mesh axis runs over, the one named last changes fastest.
Arguments:
- query_states: bfloat16 [64, 1024, 5120], P('dp', 'ctx'), may hold values from -64 to 64
- key_states: bfloat16 [64, 1024, 1024], P('dp', 'ctx'), may hold values from -16 to 16
- out_grad: bfloat16 [64, 1024, 5120], P('dp', 'ctx'), may hold values from -6 to 6
- layer_input: bfloat16 [64, 1024, 5120], P('dp', 'ctx'), may hold values from -6 to 6
- block_mask: int32 [64, 8, 8], P('dp'), may hold values from 0 to 1, as said below
Outputs:
- value_grad: bfloat16 [64, 1024, 1024], P('dp', 'ctx')
- weight_grad: float32 [5120, 1024], P('dp', 'ctx')
Inputs may be any that keep to these rules, and one draw needn't show every extreme that they name: block_mask[b] is the ancestor relation of a forest over the 8 blocks of sequence b: entry (r, c) is 1 exactly when block c is block r or an ancestor of it, and every block's parent comes before it.
All inputs are finite; a program needn't handle non-finite values.
Results may differ from a plain program's by a relative error of at most 0.0048.
Values may be sent and summed in bfloat16 or wider, within the bound.
A program may use at most 64 MiB of HBM per device.

v0:
```python
import math

import jax
import jax.numpy as jnp
from jax import lax
from jax.sharding import PartitionSpec as P

MODEL_WIDTH = 5120
HEAD_SIZE = 128
BLK = 128
GROUP = 5


def body(query_states, key_states, out_grad, layer_input, block_mask):
    inv_root = 1.0 / math.sqrt(HEAD_SIZE)
    q_heads, g_heads, k_heads = (
        lax.all_to_all(query_states, "ctx", split_axis=2, concat_axis=1, tiled=True),
        lax.all_to_all(out_grad, "ctx", split_axis=2, concat_axis=1, tiled=True),
        lax.all_to_all(key_states, "ctx", split_axis=2, concat_axis=1, tiled=True),
    )
    seq = q_heads.shape[1]
    row_span = min(512, seq)
    positions = jnp.arange(seq)
    kv_total = jnp.zeros((seq, HEAD_SIZE), jnp.float32)
    for row_first in range(0, seq, row_span):
        block_rows = block_mask[0, row_first // BLK : (row_first + row_span) // BLK, : seq // BLK]
        expanded = jnp.repeat(jnp.repeat(block_rows, BLK, axis=0), BLK, axis=1) == 1
        visible = expanded & (
            positions[None, :seq] <= positions[row_first : row_first + row_span, None]
        )
        key_block = k_heads[0, :seq, 0:HEAD_SIZE]
        for q_index in range(GROUP):
            column = q_index * HEAD_SIZE
            queries = q_heads[0, row_first : row_first + row_span, column : column + HEAD_SIZE]
            scores = (
                jnp.einsum("qd,kd->qk", queries, key_block, preferred_element_type=jnp.float32)
                * inv_root
            )
            masked = jnp.where(visible, scores, -jnp.inf)
            row_max = jnp.max(masked, axis=1, keepdims=True)
            log_total = row_max + jnp.log(jnp.sum(jnp.exp(masked - row_max), axis=1, keepdims=True))
            weights = jnp.exp(masked - log_total).astype(jnp.bfloat16)
            grad_rows = g_heads[0, row_first : row_first + row_span, column : column + HEAD_SIZE]
            contrib = jnp.einsum(
                "qk,qd->kd", weights, grad_rows, preferred_element_type=jnp.float32
            )
            kv_total = kv_total.at[:seq].add(contrib)
    value_heads = kv_total.astype(jnp.bfloat16)
    value_grad = lax.all_to_all(value_heads[None], "ctx", split_axis=1, concat_axis=2, tiled=True)
    product = lax.dot_general(
        lax.all_gather(layer_input, "ctx", axis=1, tiled=True)[0],
        value_heads,
        (((0,), (0,)), ((), ())),
        preferred_element_type=jnp.float32,
    )
    n_dp = lax.axis_size("dp")
    summed = lax.psum(product, "dp")
    row_share = MODEL_WIDTH // n_dp
    summed = lax.dynamic_slice_in_dim(summed, lax.axis_index("dp") * row_share, row_share, 0)
    return (value_grad, summed / n_dp)


def solution(mesh):
    in_specs = (
        P("dp", "ctx", None),
        P("dp", "ctx", None),
        P("dp", "ctx", None),
        P("dp", "ctx", None),
        P("dp", None, None),
    )
    out_specs = (P("dp", "ctx", None), P("dp", "ctx"))
    return jax.shard_map(body, mesh=mesh, in_specs=in_specs, out_specs=out_specs, check_vma=False)
```

profile of v0, /device:TPU:1, one launch (start us, length us, event | category | flops | bytes accessed | tf_op | source)
XLA Modules:
  0.0 831.7 jit_solution(2058777437529279904)
XLA Ops:
  7.2 0.7 all-gather.2.cloned.1.call-update
  7.9 1.3 copy.38
  9.2 0.5 broadcast.242
  9.7 2.2 reduce.30
  11.9 0.8 reshape.384
  12.7 13.3 %all-to-all-start.1 = ((bf16[8,2,8192]{2,1,0:T(2,128)(2,1)}), bf16[8,2,8192]{2,1,0:T(2,128)(2,1)S(1)}, u32[]{:S(2)}, u32[]{:S(2)}) async-start(bf16[8,2,8192]{2,1,0:T(2,128)(2,1)} %reshape.384), calls=%async_computation.1 | async-start | bytes 524288 | tf_op jit(solution)/shard_map/all_to_all | solution.py:19
  26.0 4.8 copy.36
  30.8 28.9 %reduce.31 = bf16[5120,128]{1,0:T(8,128)(2,1)} reduce(bf16[5120,1,128]{2,1,0:T(2,128)(2,1)S(1)} %bitcast.159, bf16[]{:T(256)} %broadcast.242), dimensions={1}, to_apply=%bitcast.118.reduce_sub_computation | reduce | bytes 2621442
  59.7 4.0 reshape.386
  63.7 9.6 %all-to-all-start = ((bf16[8,2,40960]{2,1,0:T(2,128)(2,1)}), bf16[8,2,40960]{2,1,0:T(2,128)(2,1)}, u32[]{:S(2)}, u32[]{:S(2)}) async-start(bf16[8,2,40960]{2,1,0:T(2,128)(2,1)} %reshape.386), calls=%async_computation | async-start | bytes 2621440 | tf_op jit(solution)/shard_map/all_to_all | solution.py:17
  73.4 4.8 copy.40
  78.2 28.9 %reduce.32 = bf16[5120,128]{1,0:T(8,128)(2,1)} reduce(bf16[5120,1,128]{2,1,0:T(2,128)(2,1)S(1)} %bitcast.160, bf16[]{:T(256)} %broadcast.242), dimensions={1}, to_apply=%bitcast.120.reduce_sub_computation | reduce | bytes 2621442
  107.1 4.0 reshape.388
  111.1 9.1 %all-to-all-start.2 = ((bf16[8,2,40960]{2,1,0:T(2,128)(2,1)}), bf16[8,2,40960]{2,1,0:T(2,128)(2,1)}, u32[]{:S(2)}, u32[]{:S(2)}) async-start(bf16[8,2,40960]{2,1,0:T(2,128)(2,1)} %reshape.388), calls=%async_computation.2 | async-start | bytes 2621440 | tf_op jit(solution)/shard_map/all_to_all | solution.py:18
  121.0 4.5 reshape.387
  125.5 1.2 copy.46
  126.7 2.4 copy.37
  129.2 67.9 %all-to-all-done.2 = bf16[8,2,40960]{2,1,0:T(2,128)(2,1)} async-done(((bf16[8,2,40960]{2,1,0:T(2,128)(2,1)}), bf16[8,2,40960]{2,1,0:T(2,128)(2,1)}, u32[]{:S(2)}, u32[]{:S(2)}) %all-to-all-start.2) | async-done | bytes 1310752 | tf_op jit(solution)/shard_map/all_to_all | solution.py:18
  197.0 4.5 reshape.389
  201.5 1.2 copy.48
  202.8 1.8 copy.41
  204.6 1.6 broadcast_in_dim.22
  206.2 0.8 fusion.21
  207.1 0.5 exponential_reduce_fusion.9
  207.6 0.8 fusion.22
  208.4 0.5 exponential_reduce_fusion.8
  209.0 0.8 fusion.23
  209.8 0.5 exponential_reduce_fusion.7
  210.3 0.8 fusion.24
  211.2 0.5 exponential_reduce_fusion.6
  211.7 0.8 fusion.25
  212.5 0.5 exponential_reduce_fusion.5
  213.1 1.8 broadcast_in_dim.25
  214.9 0.8 fusion.26
  215.7 0.5 exponential_reduce_fusion.4
  216.2 0.8 fusion.27
  217.1 0.5 exponential_reduce_fusion.3
  217.6 0.8 fusion.28
  218.4 0.5 exponential_reduce_fusion.2
  219.0 0.8 fusion.29
  219.8 0.5 exponential_reduce_fusion.1
  220.3 0.8 fusion.30
  221.2 0.5 exponential_reduce_fusion
  221.8 0.6 fusion.8
  222.4 0.6 convolution_add_fusion.8
  223.1 0.6 convolution_add_fusion.7
  223.7 0.6 convolution_add_fusion.6
  224.4 0.6 convolution_add_fusion.5
  225.0 0.6 convolution_add_fusion.4
  225.7 0.6 convolution_add_fusion.3
  226.3 0.6 convolution_add_fusion.2
  227.0 0.6 convolution_add_fusion.1
  227.6 0.7 fusion.7
  228.3 43.5 %all-gather.2.cloned.1.call-done = bf16[1,1024,5120]{2,1,0:T(8,128)(2,1)} async-done(((bf16[1,128,5120]{2,1,0:T(8,128)(2,1)}), bf16[1,1024,5120]{2,1,0:T(8,128)(2,1)}) %all-gather.2.cloned.1.call-update) | async-done | bytes 10485776 | tf_op jit(solution)/shard_map/all_gather | solution.py:51
  271.8 7.3 fusion.2
  279.1 0.4 copy.75
  279.6 2.2 reduce.33
  281.8 0.8 reshape.390
  282.5 3.6 all-to-all-start.3
  286.1 10.0 %all-to-all-done.3 = bf16[8,2,8192]{2,1,0:T(2,128)(2,1)S(1)} async-done(((bf16[8,2,8192]{2,1,0:T(2,128)(2,1)}), bf16[8,2,8192]{2,1,0:T(2,128)(2,1)S(1)}, u32[]{:S(2)}, u32[]{:S(2)}) %all-to-all-start.3) | async-done | bytes 262176 | tf_op jit(solution)/shard_map/all_to_all | solution.py:49
  296.7 0.9 copy.44
  297.5 525.4 %all-reduce.2.cloned.1.call-done = f32[5120,128]{0,1:T(8,128)} async-done(((f32[5120,128]{0,1:T(8,128)}), f32[5120,128]{0,1:T(8,128)}) %all-reduce.2.cloned.1.call-update) | async-done | bytes 2621456 | tf_op jit(solution)/shard_map/psum | solution.py:57
  822.9 1.0 dynamic-slice_multiply_fusion
  823.9 0.7 copy.45
  (32 shorter events, 1.4 us)
Async XLA Ops:
  7.2 264.6 %all-gather.2.cloned.1.call-start = ((), (), s32[]{:S(2)}) async-start(), calls=%async_computation.4 | async-start | bytes 11796480 | tf_op jit(solution)/shard_map/all_gather | solution.py:51
  12.7 51.1 %all-to-all-start.1 = ((bf16[8,2,8192]{2,1,0:T(2,128)(2,1)}), bf16[8,2,8192]{2,1,0:T(2,128)(2,1)S(1)}, u32[]{:S(2)}, u32[]{:S(2)}) async-start(bf16[8,2,8192]{2,1,0:T(2,128)(2,1)} %reshape.384), calls=%async_computation.1 | async-start | bytes 524288 | tf_op jit(solution)/shard_map/all_to_all | solution.py:19
  63.7 47.4 %all-to-all-start = ((bf16[8,2,40960]{2,1,0:T(2,128)(2,1)}), bf16[8,2,40960]{2,1,0:T(2,128)(2,1)}, u32[]{:S(2)}, u32[]{:S(2)}) async-start(bf16[8,2,40960]{2,1,0:T(2,128)(2,1)} %reshape.386), calls=%async_computation | async-start | bytes 2621440 | tf_op jit(solution)/shard_map/all_to_all | solution.py:17
  107.1 13.4 %copy-start.1 = (s32[1,8,8]{2,1,0:T(8,128)S(1)}, s32[1,8,8]{2,1,0:T(8,128)}, u32[]{:S(2)}) copy-start(s32[1,8,8]{2,1,0:T(8,128)} %param.49) | copy-start | bytes 772
  111.1 85.9 %all-to-all-start.2 = ((bf16[8,2,40960]{2,1,0:T(2,128)(2,1)}), bf16[8,2,40960]{2,1,0:T(2,128)(2,1)}, u32[]{:S(2)}, u32[]{:S(2)}) async-start(bf16[8,2,40960]{2,1,0:T(2,128)(2,1)} %reshape.388), calls=%async_computation.2 | async-start | bytes 2621440 | tf_op jit(solution)/shard_map/all_to_all | solution.py:18
  120.2 702.8 %all-reduce.2.cloned.1.call-start = ((), (), s32[]{:S(2)}) async-start(), calls=%async_computation.5 | async-start | bytes 5242880 | tf_op jit(solution)/shard_map/psum | solution.py:57
  202.8 3.5 copy-start
  282.5 13.6 %all-to-all-start.3 = ((bf16[8,2,8192]{2,1,0:T(2,128)(2,1)}), bf16[8,2,8192]{2,1,0:T(2,128)(2,1)S(1)}, u32[]{:S(2)}, u32[]{:S(2)}) async-start(bf16[8,2,8192]{2,1,0:T(2,128)(2,1)} %reshape.390), calls=%async_computation.3 | async-start | bytes 524288 | tf_op jit(solution)/shard_map/all_to_all | solution.py:49
Sparse Core Ops, SparseCore 0:
  11.2 260.5 all-gather.1
  279.3 543.6 all-reduce.1
where the time goes:
time: 838 us; the launch traced here: 832 us
  waiting for transfers between devices  647 us (77%)
  other arithmetic  68.4 us (8%)
  local copies, waits for them, and re-layouts  43.2 us (5%)
  starting transfers between devices  35.8 us (4%)
  matrix products  22.2 us (3%)
  between operations  14.7 us (2%)
    psum x1, waiting for transfers between devices, body(): summed = lax.psum(product, 'dp')  525 us
    all_to_all x1, waiting for transfers between devices, body(): lax.all_to_all(out_grad, 'ctx', split_axis=2, concat_axis=1, tiled=True)  67.9 us
    unnamed x4, other arithmetic  62.2 us
    all_gather x1, waiting for transfers between devices, body(): lax.all_gather(layer_input, 'ctx', axis=1, tiled=True)[0]  43.5 us
    unnamed x22, local copies, waits for them, and re-layouts  34.7 us
  transfers between devices with their start and end apart: 6, of which 4 were waited for; matrix products, arithmetic and copies ran while one was open for 15% of the time, Pallas kernels for 0%

commit v1 on v0

v1 whole, which is shorter than its diff:
```python
import functools
import math

import jax
import jax.numpy as jnp
from jax import lax
from jax.experimental import pallas as pl
from jax.experimental.pallas import tpu as pltpu
from jax.sharding import PartitionSpec as P

HEAD = 128
GROUP = 5
BF16 = jnp.bfloat16
F32 = jnp.float32
MESH = pl.DeviceIdType.MESH
HIDDEN = -1e30


def kernel(
    q_ref, k_ref, g_ref, x_ref, mask_ref, vgrad_ref, wgrad_ref,
    qb, gb, kb, xb, xt, bias, vacc, vsend, vrecv, v2, ca, cb, ra, rb, sa, sb, fin,
    own_sem, k_ss, k_rs, q_ss, q_rs, g_ss, g_rs, x_ss, x_rs, z_ss, z_rs, a_ss, a_rs,
    f_ss, f_rs, ra_ss, ra_rs, rb_ss, rb_rs, fin_ss, fin_rs,
):
    d = lax.axis_index("dp")
    t = lax.axis_index("ctx")
    core = lax.rem(d, 2)
    zl = lax.rem(lax.div(d, 2), 4)
    y = lax.div(d, 8)
    x = lax.div(t, 2)
    zh = lax.rem(t, 2)
    z = zh * 4 + zl
    d_core = d + 1 - 2 * core
    y_odd = lax.rem(y, 2)
    z_odd = lax.rem(z, 2)

    def place(px, py, pz, pc):
        return ((py * 4 + lax.rem(pz, 4)) * 2 + pc, px * 2 + lax.div(pz, 4))

    def mine(px, py, pz, pc):
        dd, tt = place(px, py, pz, pc)
        return jnp.logical_and(dd == d, tt == t)

    def send(src, dst, ss, rs, to):
        return pltpu.make_async_remote_copy(
            src_ref=src, dst_ref=dst, send_sem=ss, recv_sem=rs, device_id=to, device_id_type=MESH
        )

    dest_a = [(lax.div(y, 2), 2 * x + core, 2 * m + y_odd, y_odd) for m in range(4)]
    dest_b = [(n, 2 * x + core, z, 1 - z_odd) for n in range(4)]
    row_block = 2 * x + core
    by_y_first = lax.rem(row_block + z, 2) == 0
    sources = [
        (
            lax.div(y, 2),
            jnp.where(by_y_first, row_block, s),
            jnp.where(by_y_first, s, z),
            y_odd,
        )
        for s in range(8)
    ]

    barrier = pltpu.get_barrier_semaphore()

    def greet(to):
        pl.semaphore_signal(barrier, inc=1, device_id=to, device_id_type=MESH)

    for o in range(1, 8):
        greet((d, lax.rem(t + o, 8)))
    for o in range(4):
        greet((d_core, lax.rem(x + o, 4) * 2 + zh))
    for o in range(1, 8):
        greet(place(x, lax.rem(y + o, 8), z, core))
        if o != 4:
            greet(place(x, y, lax.rem(z + o, 8), core))
    for source in sources:
        @pl.when(jnp.logical_not(mine(*source)))
        def _():
            greet(place(*source))
    expected = 24
    for dest in dest_a + dest_b:
        expected = expected + jnp.where(mine(*dest), 0, 1)
    pl.semaphore_wait(barrier, expected)

    k_out, q_out, g_out, own = [], [], [], []
    for j in range(2):
        def cols(head_x, per_x, width):
            return pl.ds(pl.multiple_of(head_x * per_x + j * width, 128), width)

        k_row, q_row, g_row = [], [], []
        for o in (4, 2, 6, 1, 7, 3, 5):
            to = lax.rem(t + o, 8)
            k_row.append(send(
                k_ref.at[0, :, cols(lax.div(to, 2), 256, 128)], kb.at[j, t],
                k_ss.at[j, o - 1], k_rs.at[j, o - 1], (d, to),
            ))
        for o in (2, 1, 3):
            tx = lax.rem(x + o, 4)
            q_row.append(send(
                q_ref.at[0, :, cols(tx, 1280, 640)], qb.at[j, x],
                q_ss.at[j, o - 1], q_rs.at[j, o - 1], (d, tx * 2 + zh),
            ))
            g_row.append(send(
                g_ref.at[0, :, cols(tx, 1280, 640)], gb.at[j, x],
                g_ss.at[j, o - 1], g_rs.at[j, o - 1], (d, tx * 2 + zh),
            ))
        own_row = [
            pltpu.make_async_copy(k_ref.at[0, :, cols(x, 256, 128)], kb.at[j, t], own_sem.at[j, 0]),
            pltpu.make_async_copy(q_ref.at[0, :, cols(x, 1280, 640)], qb.at[j, x], own_sem.at[j, 1]),
            pltpu.make_async_copy(g_ref.at[0, :, cols(x, 1280, 640)], gb.at[j, x], own_sem.at[j, 2]),
        ]
        for copy in k_row + q_row + g_row + own_row:
            copy.start()
        k_out.append(k_row)
        q_out.append(q_row)
        g_out.append(g_row)
        own.append(own_row)

    key_pos = lax.broadcasted_iota(jnp.int32, (128, 128), 0)
    query_pos = lax.broadcasted_iota(jnp.int32, (128, 128), 1)
    for k in range(4):
        for c in range(2 * k + 2):
            seen = jnp.where(mask_ref[0, 2 * k + zh, c] == 1, 0.0, HIDDEN)
            behind = key_pos + c * 128 <= query_pos + (2 * k + zh) * 128
            bias[k, c * 128 : (c + 1) * 128] = jnp.where(behind, seen, HIDDEN)
    vacc[...] = jnp.zeros_like(vacc)

    scale = math.log2(math.e) / math.sqrt(HEAD)

    def attend(j):
        for k in range(4):
            n = (2 * k + 2) * 128
            keys = kb[j, 0 : 2 * k + 2].reshape(n, 128)

            @pl.loop(0, GROUP)
            def _(h):
                col = pl.ds(pl.multiple_of(h * 128, 128), 128)
                s = lax.dot_general(
                    keys, qb[j, k, :, col], (((1,), (1,)), ((), ())), preferred_element_type=F32
                )
                s = s * scale + bias[k, 0:n]
                p = jnp.exp2(s - jnp.max(s, axis=0, keepdims=True))
                w = (p * (1.0 / jnp.sum(p, axis=0, keepdims=True))).astype(BF16)
                vacc[j, 0:n] += jnp.dot(w, gb[j, k, :, col], preferred_element_type=F32)

    z_out, x_out = [], []
    for j in range(2):
        for copy in k_out[j] + q_out[j] + g_out[j]:
            copy.wait_recv()
        for copy in own[j]:
            copy.wait()
        if j == 0:
            for o in (4, 2, 6, 5, 3, 7, 1):
                tx, tc = lax.rem(x + o // 2, 4), lax.rem(core + o % 2, 2)
                x_out.append(send(
                    x_ref.at[0, :, pl.ds(pl.multiple_of(tx * 1280 + tc * 640, 128), 640)],
                    xb.at[core, x], x_ss.at[o - 1], x_rs.at[o - 1], (d - core + tc, tx * 2 + zh),
                ))
            own_x = pltpu.make_async_copy(
                x_ref.at[0, :, pl.ds(pl.multiple_of(x * 1280 + core * 640, 128), 640)],
                xb.at[core, x], own_sem.at[0, 3],
            )
            for copy in x_out + [own_x]:
                copy.start()
        attend(j)
        for k in range(4):
            far = pl.ds(pl.multiple_of((2 * k + 1 - zh) * 128, 128), 128)
            vsend[j, k * 128 : (k + 1) * 128] = vacc[j, far].astype(BF16)
        z_out.append(send(
            vsend.at[j], vrecv.at[j], z_ss.at[j], z_rs.at[j], (d, x * 2 + 1 - zh)
        ))
        z_out[j].start()

    a_out = []
    for j in range(2):
        z_out[j].wait_recv()
        for k in range(4):
            near = pl.ds(pl.multiple_of((2 * k + zh) * 128, 128), 128)
            rows = pl.ds(k * 128, 128)
            v2[core, 2 * x + j, rows] = (vacc[j, near] + vrecv[j, rows].astype(F32)).astype(BF16)
        mine_v = v2.at[core, 2 * x + j]
        row = []
        for o in (2, 1, 3):
            row.append(send(
                mine_v, mine_v, a_ss.at[j, o], a_rs.at[j, o], (d, lax.rem(x + o, 4) * 2 + zh)
            ))
        row.append(send(mine_v, mine_v, f_ss.at[j, 0], f_rs.at[j, 0], (d_core, t)))
        for copy in row:
            copy.start()
        a_out.append(row)

    for copy in x_out:
        copy.wait_recv()
    own_x.wait()
    for i in range(8):
        xt[:, i * 128 : (i + 1) * 128] = jnp.transpose(xb[i // 4, i % 4])

    f_out = []
    for j in range(2):
        for o, copy in zip((2, 1, 3), a_out[j]):
            copy.wait_recv()
            block = v2.at[core, 2 * lax.rem(x + 4 - o, 4) + j]
            f_out.append(send(block, block, f_ss.at[j, o], f_rs.at[j, o], (d_core, t)))
            f_out[-1].start()
    for g in range(8):
        vgrad_ref[0, :, g * 128 : (g + 1) * 128] = v2[core, g, pl.ds(pl.multiple_of(x * 128, 128), 128)]
    for copy in f_out + [row[3] for row in a_out]:
        copy.wait_recv()

    @pl.loop(0, 4)
    def _(xx):
        for zz in range(4):
            rows = slice(zz * 160, (zz + 1) * 160)
            total = jnp.zeros((160, 256), F32)
            for cs in range(2):
                values = jnp.concatenate([v2[cs, 2 * xx], v2[cs, 2 * xx + 1]], axis=1)
                total += jnp.dot(
                    xt[rows, cs * 512 : (cs + 1) * 512], values, preferred_element_type=F32
                )
            total = total.astype(BF16)
            for cc in range(2):
                for hh in range(2):
                    block = total[cc * 80 : (cc + 1) * 80, hh * 128 : (hh + 1) * 128]
                    if (cc + zz) % 2 == 0:
                        ca[2 * xx + cc, hh * 2 + zz // 2] = block
                    else:
                        cb[hh * 4 + zz, xx] = block

    ra_out, rb_out = [], []
    for o in (4, 3, 5, 2, 6, 1, 7):
        ty, tz = lax.rem(y + o, 8), lax.rem(z + o, 8)
        ra_out.append(send(
            ca.at[ty], ra.at[y], ra_ss.at[o - 1], ra_rs.at[o - 1], place(x, ty, z, core)
        ))
        rb_out.append(send(
            cb.at[tz], rb.at[z], rb_ss.at[o - 1], rb_rs.at[o - 1], place(x, y, tz, core)
        ))
        ra_out[-1].start()
        rb_out[-1].start()
    for copy in ra_out + rb_out:
        copy.wait_recv()
    for own_part, parts, me, out in ((ca, ra, y, sa), (cb, rb, z, sb)):
        for m in range(4):
            total = own_part[me, m].astype(F32)
            for o in range(1, 8):
                total += parts[lax.rem(me + o, 8), m].astype(F32)
            out[m] = total.astype(BF16)

    fin_out = []
    for i, dest in enumerate(dest_a + dest_b):
        src = (sa if i < 4 else sb).at[i % 4]
        slot = z if i < 4 else y
        copy = send(src, fin.at[slot], fin_ss.at[i], fin_rs.at[slot], place(*dest))
        fin_out.append((copy, dest))
        here = mine(*dest)

        @pl.when(here)
        def _():
            fin[slot] = src[...]

        @pl.when(jnp.logical_not(here))
        def _():
            copy.start()

    total = jnp.zeros((80, 128), F32)
    for s, source in enumerate(sources):
        @pl.when(jnp.logical_not(mine(*source)))
        def _():
            send(sa.at[0], fin.at[s], fin_ss.at[0], fin_rs.at[s], place(*source)).wait_recv()

        total += fin[s].astype(F32)
    wgrad_ref[...] = total * (1.0 / 64.0)

    for j in range(2):
        for copy in k_out[j] + q_out[j] + g_out[j] + a_out[j]:
            copy.wait_send()
    for copy in x_out + z_out + f_out + ra_out + rb_out:
        copy.wait_send()
    for copy, dest in fin_out:
        @pl.when(jnp.logical_not(mine(*dest)))
        def _():
            copy.wait_send()


def body(query_states, key_states, out_grad, layer_input, block_mask):
    vmem, dma = pltpu.VMEM, pltpu.SemaphoreType.DMA
    return pl.pallas_call(
        kernel,
        out_shape=(
            jax.ShapeDtypeStruct((1, 128, 1024), BF16),
            jax.ShapeDtypeStruct((80, 128), F32),
        ),
        in_specs=[pl.BlockSpec(memory_space=pl.ANY)] * 4 + [pl.BlockSpec(memory_space=pltpu.SMEM)],
        out_specs=(pl.BlockSpec(memory_space=vmem), pl.BlockSpec(memory_space=vmem)),
        scratch_shapes=[
            vmem((2, 4, 128, 640), BF16),
            vmem((2, 4, 128, 640), BF16),
            vmem((2, 8, 128, 128), BF16),
            vmem((2, 4, 128, 640), BF16),
            vmem((640, 1024), BF16),
            vmem((4, 1024, 128), F32),
            vmem((2, 1024, 128), F32),
            vmem((2, 512, 128), BF16),
            vmem((2, 512, 128), BF16),
            vmem((2, 8, 512, 128), BF16),
            vmem((8, 4, 80, 128), BF16),
            vmem((8, 4, 80, 128), BF16),
            vmem((8, 4, 80, 128), BF16),
            vmem((8, 4, 80, 128), BF16),
            vmem((4, 80, 128), BF16),
            vmem((4, 80, 128), BF16),
            vmem((8, 80, 128), BF16),
            dma((2, 4)),
            dma((2, 7)), dma((2, 7)), dma((2, 3)), dma((2, 3)), dma((2, 3)), dma((2, 3)),
            dma((7,)), dma((7,)), dma((2,)), dma((2,)), dma((2, 4)), dma((2, 4)),
            dma((2, 4)), dma((2, 4)), dma((7,)), dma((7,)), dma((7,)), dma((7,)),
            dma((8,)), dma((8,)),
        ],
        compiler_params=pltpu.CompilerParams(
            collective_id=0, has_side_effects=True, vmem_limit_bytes=48 * 2**20
        ),
        name="value_path",
    )(query_states, key_states, out_grad, layer_input, block_mask)


def solution(mesh):
    in_specs = (
        P("dp", "ctx", None),
        P("dp", "ctx", None),
        P("dp", "ctx", None),
        P("dp", "ctx", None),
        P("dp", None, None),
    )
    out_specs = (P("dp", "ctx", None), P("dp", "ctx"))
    return jax.shard_map(body, mesh=mesh, in_specs=in_specs, out_specs=out_specs, check_vma=False)
```

time: 838 us -> 121 us (0.14)
  the two profiles are of different devices: /device:TPU:1 before, /device:TPU:48 now
where the time goes in v1:
time: 121 us; the launch traced here: 120 us
  Pallas kernels  113 us (93%)
  local copies, waits for them, and re-layouts  6.9 us (6%)
    pallas_call x1, Pallas kernels, body(): pl.pallas_call(kernel, out_shape=(jax.ShapeDtypeStruct((1, 128, 1024), BF...  113 us
    unnamed x12, local copies, waits for them, and re-layouts  6.9 us

profile of v1, /device:TPU:48, one launch (start us, length us, event | category | flops | bytes accessed | tf_op | source)
XLA Modules:
  0.0 120.3 jit_solution(3629271578936763437)
XLA Ops:
  0.6 0.0 copy-start
  0.6 1.3 %copy-done = bf16[1,128,5120]{2,1,0:T(8,128)(2,1)S(1)} copy-done((bf16[1,128,5120]{2,1,0:T(8,128)(2,1)S(1)}, bf16[1,128,5120]{2,1,0:T(8,128)(2,1)}, u32[]{:S(2)}) %copy-start) | copy-done | bytes 1310744
  1.9 0.0 copy-start.1
  2.0 1.3 %copy-done.1 = bf16[1,128,5120]{2,1,0:T(8,128)(2,1)S(1)} copy-done((bf16[1,128,5120]{2,1,0:T(8,128)(2,1)S(1)}, bf16[1,128,5120]{2,1,0:T(8,128)(2,1)}, u32[]{:S(2)}) %copy-start.1) | copy-done | bytes 1310744
  3.3 0.0 copy-start.2
  3.3 1.3 %copy-done.2 = bf16[1,128,5120]{2,1,0:T(8,128)(2,1)S(1)} copy-done((bf16[1,128,5120]{2,1,0:T(8,128)(2,1)S(1)}, bf16[1,128,5120]{2,1,0:T(8,128)(2,1)}, u32[]{:S(2)}) %copy-start.2) | copy-done | bytes 1310744
  4.6 0.0 copy-start.3
  4.6 0.9 copy-done.3
  5.5 0.0 copy-start.4
  5.5 0.7 copy-done.4
  6.2 112.8 %value_path.1 = (bf16[1,128,1024]{2,1,0:T(8,128)(2,1)S(1)}, f32[80,128]{1,0:T(8,128)S(1)}) custom-call(bf16[1,128,5120]{2,1,0:T(8,128)(2,1)S(1)} %copy-done, bf16[1,128,1024]{2,1,0:T(8,128)(2,1)S(1)} %copy-done.3, bf16[1,128,5120]{2,1,0:T(8,128)(2,1)S(1)} %copy-done.1, bf16[1,128,5120]{2,1,0:T(8,128)(2,1)S(1)} %copy-done.2, s32[1,8,8]{2,1,0:T(8,128)S(1)} %copy-done.4), custom_call_target="tpu_custom_call" | custom-call | tf_op jit(solution)/shard_map/value_path/pallas_call | solution.py:287
  119.0 0.7 copy.9
  119.7 0.6 copy.10
Async XLA Ops:
  0.6 1.3 %copy-start = (bf16[1,128,5120]{2,1,0:T(8,128)(2,1)S(1)}, bf16[1,128,5120]{2,1,0:T(8,128)(2,1)}, u32[]{:S(2)}) copy-start(bf16[1,128,5120]{2,1,0:T(8,128)(2,1)} %q_ref.1) | copy-start | bytes 3932164
  1.9 1.3 %copy-start.1 = (bf16[1,128,5120]{2,1,0:T(8,128)(2,1)S(1)}, bf16[1,128,5120]{2,1,0:T(8,128)(2,1)}, u32[]{:S(2)}) copy-start(bf16[1,128,5120]{2,1,0:T(8,128)(2,1)} %g_ref.1) | copy-start | bytes 3932164
  3.3 1.3 %copy-start.2 = (bf16[1,128,5120]{2,1,0:T(8,128)(2,1)S(1)}, bf16[1,128,5120]{2,1,0:T(8,128)(2,1)}, u32[]{:S(2)}) copy-start(bf16[1,128,5120]{2,1,0:T(8,128)(2,1)} %x_ref.1) | copy-start | bytes 3932164
  4.6 0.9 copy-start.3
  5.5 0.7 copy-start.4

commit v2 on v0

v2 whole, which is shorter than its diff:
```python
import functools
import math

import jax
import jax.numpy as jnp
from jax import lax
from jax.experimental import pallas as pl
from jax.experimental.pallas import tpu as pltpu
from jax.sharding import PartitionSpec as P

HEAD = 128
GROUP = 5
BF16 = jnp.bfloat16
F32 = jnp.float32
MESH = pl.DeviceIdType.MESH
HIDDEN = -1e30
X_AT = 8
SHARE_AT = 8
AHEAD = 3


def kernel(
    q_ref, k_ref, g_ref, x_ref, mask_ref, vgrad_ref, parts_ref,
    qb, gb, kb, xin, xtl, xt, bias, vacc, vsend, vrecv, v2, ca, cb, ra, rb, sa, sb, fin,
    own_sem, q_own, g_own, k_ss, k_rs, q_ss, q_rs, g_ss, g_rs, x_ss, x_rs, z_ss, z_rs, a_ss, a_rs,
    f_ss, f_rs, ra_ss, ra_rs, rb_ss, rb_rs, fin_ss, fin_rs,
):
    d = lax.axis_index("dp")
    t = lax.axis_index("ctx")
    core = lax.rem(d, 2)
    zl = lax.rem(lax.div(d, 2), 4)
    y = lax.div(d, 8)
    x = lax.div(t, 2)
    zh = lax.rem(t, 2)
    z = zh * 4 + zl
    d_core = d + 1 - 2 * core
    y_odd = lax.rem(y, 2)
    zl_odd = lax.rem(zl, 2)

    def place(px, py, pz, pc):
        return ((py * 4 + lax.rem(pz, 4)) * 2 + pc, px * 2 + lax.div(pz, 4))

    def mine(px, py, pz, pc):
        dd, tt = place(px, py, pz, pc)
        return jnp.logical_and(dd == d, tt == t)

    def send(src, dst, ss, rs, to):
        return pltpu.make_async_remote_copy(
            src_ref=src, dst_ref=dst, send_sem=ss, recv_sem=rs, device_id=to, device_id_type=MESH
        )

    x_in = pltpu.make_async_copy(x_ref.at[0], xin, own_sem.at[0, 3])
    x_in.start()

    dest = []
    for j in range(2):
        for m in range(2):
            dest.append((2 * m + y_odd, y, j * 4 + x, core))
        for n in range(2):
            dest.append((zl, 4 * zh + 2 * n + 1 - zl_odd, j * 4 + x, core))
    y_first = lax.rem(x + y, 2) == 0
    half_z = lax.div(y, 4) * 4 + x
    sources = [
        (zl, jnp.where(y_first, y, s), jnp.where(y_first, s, half_z), core) for s in range(8)
    ]

    sent, open_recv = [], []

    def go(*copies):
        for copy in copies:
            copy.start()
            sent.append(copy)
            open_recv.append(copy)

    def arrive(*copies):
        for copy in copies:
            copy.wait_recv()
            open_recv[:] = [other for other in open_recv if other is not copy]

    def finish():
        for copy in open_recv:
            copy.wait_recv()
        for copy in sent:
            copy.wait_send()

    barrier = pltpu.get_barrier_semaphore()

    def greet(to):
        pl.semaphore_signal(barrier, inc=1, device_id=to, device_id_type=MESH)

    for o in range(1, 8):
        greet((d, lax.rem(t + o, 8)))
    for o in range(4):
        greet((d_core, lax.rem(x + o, 4) * 2 + zh))
    for o in range(1, 8):
        greet(place(x, lax.rem(y + o, 8), z, core))
        if o != 4:
            greet(place(x, y, lax.rem(z + o, 8), core))
    for source in sources:
        @pl.when(jnp.logical_not(mine(*source)))
        def _():
            greet(place(*source))
    expected = 24
    for to in dest:
        expected = expected + jnp.where(mine(*to), 0, 1)
    pl.semaphore_wait(barrier, expected)

    k_out = [[], []]

    def send_keys(j):
        for o in (4, 2, 6, 1, 7, 3, 5):
            to = lax.rem(t + o, 8)
            columns = pl.ds(pl.multiple_of(lax.div(to, 2) * 256 + j * 128, 128), 128)
            k_out[j].append(send(
                k_ref.at[0, :, columns], kb.at[j, t],
                k_ss.at[j, o - 1], k_rs.at[j, o - 1], (d, to),
            ))
        go(*k_out[j])
        columns = pl.ds(pl.multiple_of(x * 256 + j * 128, 128), 128)
        pltpu.make_async_copy(k_ref.at[0, :, columns], kb.at[j, t], own_sem.at[j, 0]).start()

    def head_sends(h):
        out = []
        for o in (2, 1, 3):
            tx = lax.rem(x + o, 4)
            columns = pl.ds(pl.multiple_of(tx * 1280 + h * 128, 128), 128)
            to = (d, tx * 2 + zh)
            out.append(send(q_ref.at[0, :, columns], qb.at[h, x], q_ss.at[h, o - 1], q_rs.at[h, o - 1], to))
            out.append(send(g_ref.at[0, :, columns], gb.at[h, x], g_ss.at[h, o - 1], g_rs.at[h, o - 1], to))
        return out

    def head_own(h):
        columns = pl.ds(pl.multiple_of(x * 1280 + h * 128, 128), 128)
        return [
            pltpu.make_async_copy(q_ref.at[0, :, columns], qb.at[h, x], q_own.at[h]),
            pltpu.make_async_copy(g_ref.at[0, :, columns], gb.at[h, x], g_own.at[h]),
        ]

    def send_head(h):
        for copy in head_sends(h) + head_own(h):
            copy.start()

    send_keys(0)
    pl.loop(0, AHEAD)(send_head)
    send_keys(1)

    key_pos = lax.broadcasted_iota(jnp.int32, (128, 128), 0)
    query_pos = lax.broadcasted_iota(jnp.int32, (128, 128), 1)
    for k in range(4):
        for c in range(2 * k + 2):
            seen = jnp.where(mask_ref[0, 2 * k + zh, c] == 1, 0.0, HIDDEN)
            behind = key_pos + c * 128 <= query_pos + (2 * k + zh) * 128
            bias[k, c * 128 : (c + 1) * 128] = jnp.where(behind, seen, HIDDEN)
    vacc[...] = jnp.zeros_like(vacc)

    scale = math.log2(math.e) / math.sqrt(HEAD)

    def attend(j, h):
        for k in range(4):
            n = (2 * k + 2) * 128
            keys = kb[j, 0 : 2 * k + 2].reshape(n, 128)
            s = lax.dot_general(
                keys, qb[h, k], (((1,), (1,)), ((), ())), preferred_element_type=F32
            )
            s = s * scale + bias[k, 0:n]
            p = jnp.exp2(s - jnp.max(s, axis=0, keepdims=True))
            w = (p * (1.0 / jnp.sum(p, axis=0, keepdims=True))).astype(BF16)
            vacc[j, 0:n] += jnp.dot(w, gb[h, k], preferred_element_type=F32)

    x_in.wait()

    @pl.loop(0, 8)
    def _(yy):
        turned = jnp.transpose(xin[:, pl.ds(pl.multiple_of(yy * 640, 128), 640)])
        for b in range(8):
            xtl[b, pl.ds(pl.multiple_of(yy * 80, 16), 80)] = turned[b * 80 : (b + 1) * 80]

    x_slot = xt.at[:, pl.ds(pl.multiple_of(core * 512 + x * 128, 128), 128)]
    own_x = pltpu.make_async_copy(xtl.at[x * 2 + core], x_slot, own_sem.at[1, 3])
    own_x.start()

    x_out = []
    for o in (4, 2, 6, 5, 3, 7, 1):
        tx, tc = lax.rem(x + o // 2, 4), lax.rem(core + o % 2, 2)
        x_out.append(send(
            xtl.at[tx * 2 + tc], x_slot,
            x_ss.at[o - 1], x_rs.at[o - 1], (d - core + tc, tx * 2 + zh),
        ))

    def send_x():
        for copy in x_out:
            copy.start()

    sent.extend(x_out)

    z_out = [
        send(vsend.at[j], vrecv.at[j], z_ss.at[j], z_rs.at[j], (d, x * 2 + 1 - zh)) for j in range(2)
    ]

    a_out, f_out = [[], []], [[], []]
    for j in range(2):
        mine_v = v2.at[core, 2 * x + j]
        for o in (2, 1, 3):
            a_out[j].append(send(
                mine_v, mine_v, a_ss.at[j, o], a_rs.at[j, o], (d, lax.rem(x + o, 4) * 2 + zh)
            ))
        f_out[j].append(send(mine_v, mine_v, f_ss.at[j, 0], f_rs.at[j, 0], (d_core, t)))

    def share(j):
        z_out[j].wait_recv()
        for k in range(4):
            near = pl.ds(pl.multiple_of((2 * k + zh) * 128, 128), 128)
            rows = pl.ds(k * 128, 128)
            v2[core, 2 * x + j, rows] = (vacc[j, near] + vrecv[j, rows].astype(F32)).astype(BF16)
        for copy in a_out[j] + f_out[j][:1]:
            copy.start()

    for j in range(2):
        arrive(*k_out[j])
        pltpu.make_async_copy(k_ref.at[0, :, 0:128], kb.at[j, t], own_sem.at[j, 0]).wait()

        @pl.loop(j * GROUP, (j + 1) * GROUP)
        def _(h):
            for copy in head_sends(h):
                copy.wait_recv()
            for copy in head_own(h):
                copy.wait()

            @pl.when(h < 2 * GROUP - AHEAD)
            def _():
                send_head(h + AHEAD)

            if j == 1:
                @pl.when(h == SHARE_AT)
                def _():
                    share(0)

                @pl.when(h == X_AT)
                def _():
                    send_x()

            attend(j, h)

        for k in range(4):
            far = pl.ds(pl.multiple_of((2 * k + 1 - zh) * 128, 128), 128)
            vsend[j, k * 128 : (k + 1) * 128] = vacc[j, far].astype(BF16)
        z_out[j].start()

    def forward(j):
        for o, copy in zip((2, 1, 3), a_out[j]):
            copy.wait_recv()
            block = v2.at[core, 2 * lax.rem(x + 4 - o, 4) + j]
            f_out[j].append(send(block, block, f_ss.at[j, o], f_rs.at[j, o], (d_core, t)))
            f_out[j][-1].start()

    def multiply(j):
        for copy in f_out[j]:
            copy.wait_recv()

        @pl.loop(0, 2)
        def _(xx):
            for r in range(4):
                rows = slice(r * 160, (r + 1) * 160)
                total = jnp.zeros((160, 256), F32)
                for cs in range(2):
                    values = jnp.concatenate([v2[cs, 4 * xx + j], v2[cs, 4 * xx + 2 + j]], axis=1)
                    total += jnp.dot(
                        xt[rows, cs * 512 : (cs + 1) * 512], values, preferred_element_type=F32
                    )
                total = total.astype(BF16)
                for cc in range(2):
                    for hh in range(2):
                        block = total[cc * 80 : (cc + 1) * 80, hh * 128 : (hh + 1) * 128]
                        if cc == hh:
                            ca[j, 2 * r + cc, xx] = block
                        else:
                            cb[j, (r // 2) * 4 + 2 * xx + hh, r % 2] = block

    ra_out, rb_out = [[], []], [[], []]

    def first_sum(j):
        for o in (4, 3, 5, 2, 6, 1, 7):
            ty, tz = lax.rem(y + o, 8), lax.rem(z + o, 8)
            ra_out[j].append(send(
                ca.at[j, ty], ra.at[j, y], ra_ss.at[j, o - 1], ra_rs.at[j, o - 1],
                place(x, ty, z, core),
            ))
            rb_out[j].append(send(
                cb.at[j, tz], rb.at[j, z], rb_ss.at[j, o - 1], rb_rs.at[j, o - 1],
                place(x, y, tz, core),
            ))
            go(ra_out[j][-1], rb_out[j][-1])

    fin_out = []

    def second_sum(j):
        arrive(*ra_out[j], *rb_out[j])
        for own_part, parts, me, out in ((ca, ra, y, sa), (cb, rb, z, sb)):
            for m in range(2):
                total = own_part[j, me, m].astype(F32)
                for o in range(1, 8):
                    total += parts[j, lax.rem(me + o, 8), m].astype(F32)
                out[j, m] = total.astype(BF16)
        for i in range(4):
            src = (sa if i < 2 else sb).at[j, i % 2]
            slot = z if i < 2 else y
            to = dest[j * 4 + i]
            copy = send(src, fin.at[slot], fin_ss.at[j * 4 + i], fin_rs.at[slot], place(*to))
            fin_out.append((copy, to))
            here = mine(*to)

            @pl.when(here)
            def _():
                fin[slot] = src[...]

            @pl.when(jnp.logical_not(here))
            def _():
                copy.start()

    forward(0)
    share(1)
    for copy in x_out:
        copy.wait_recv()
    own_x.wait()
    multiply(0)
    first_sum(0)
    forward(1)
    for g in range(8):
        vgrad_ref[0, :, g * 128 : (g + 1) * 128] = v2[core, g, pl.ds(pl.multiple_of(x * 128, 128), 128)]
    multiply(1)
    first_sum(1)
    second_sum(0)
    second_sum(1)

    for s, source in enumerate(sources):
        @pl.when(jnp.logical_not(mine(*source)))
        def _():
            send(sa.at[0, 0], fin.at[s], fin_ss.at[0], fin_rs.at[s], place(*source)).wait_recv()

        parts_ref[s] = fin[s]

    finish()
    for copy in z_out + a_out[0] + a_out[1] + f_out[0] + f_out[1]:
        copy.wait_send()

    @pl.loop(0, 2 * GROUP)
    def _(h):
        for copy in head_sends(h):
            copy.wait_send()

    for copy, to in fin_out:
        @pl.when(jnp.logical_not(mine(*to)))
        def _():
            copy.wait_send()


def add_parts(values_ref, parts_ref, vgrad_ref, wgrad_ref):
    vgrad_ref[...] = values_ref[...]
    total = parts_ref[0].astype(F32)
    for s in range(1, 8):
        total += parts_ref[s].astype(F32)
    wgrad_ref[...] = total * (1.0 / 64.0)


def body(query_states, key_states, out_grad, layer_input, block_mask):
    vmem, dma = pltpu.VMEM, pltpu.SemaphoreType.DMA
    values, parts = pl.pallas_call(
        kernel,
        out_shape=(
            jax.ShapeDtypeStruct((1, 128, 1024), BF16),
            jax.ShapeDtypeStruct((8, 80, 128), BF16),
        ),
        in_specs=[pl.BlockSpec(memory_space=pltpu.HBM)] * 4 + [pl.BlockSpec(memory_space=pltpu.SMEM)],
        out_specs=(pl.BlockSpec(memory_space=vmem), pl.BlockSpec(memory_space=vmem)),
        scratch_shapes=[
            vmem((10, 4, 128, 128), BF16),
            vmem((10, 4, 128, 128), BF16),
            vmem((2, 8, 128, 128), BF16),
            vmem((128, 5120), BF16),
            vmem((8, 640, 128), BF16),
            vmem((640, 1024), BF16),
            vmem((4, 1024, 128), F32),
            vmem((2, 1024, 128), F32),
            vmem((2, 512, 128), BF16),
            vmem((2, 512, 128), BF16),
            vmem((2, 8, 512, 128), BF16),
            vmem((2, 8, 2, 80, 128), BF16),
            vmem((2, 8, 2, 80, 128), BF16),
            vmem((2, 8, 2, 80, 128), BF16),
            vmem((2, 8, 2, 80, 128), BF16),
            vmem((2, 2, 80, 128), BF16),
            vmem((2, 2, 80, 128), BF16),
            vmem((8, 80, 128), BF16),
            dma((2, 4)),
            dma((10,)), dma((10,)),
            dma((2, 7)), dma((2, 7)), dma((10, 3)), dma((10, 3)), dma((10, 3)), dma((10, 3)),
            dma((7,)), dma((7,)), dma((2,)), dma((2,)), dma((2, 4)), dma((2, 4)),
            dma((2, 4)), dma((2, 4)), dma((2, 7)), dma((2, 7)), dma((2, 7)), dma((2, 7)),
            dma((8,)), dma((8,)),
        ],
        compiler_params=pltpu.CompilerParams(
            collective_id=0, has_side_effects=True, vmem_limit_bytes=60 * 2**20
        ),
        name="value_path",
    )(query_states, key_states, out_grad, layer_input, block_mask)
    return pl.pallas_call(
        add_parts,
        out_shape=(
            jax.ShapeDtypeStruct((1, 128, 1024), BF16),
            jax.ShapeDtypeStruct((80, 128), F32),
        ),
        name="add_parts",
    )(values, parts)


def solution(mesh):
    in_specs = (
        P("dp", "ctx", None),
        P("dp", "ctx", None),
        P("dp", "ctx", None),
        P("dp", "ctx", None),
        P("dp", None, None),
    )
    out_specs = (P("dp", "ctx", None), P("dp", "ctx"))
    return jax.shard_map(body, mesh=mesh, in_specs=in_specs, out_specs=out_specs, check_vma=False)
```

time: 838 us -> 106 us (0.13)
  the two profiles are of different devices: /device:TPU:1 before, /device:TPU:15 now
where the time goes in v2:
time: 106 us; the launch traced here: 105 us
  Pallas kernels  105 us (99%)
    pallas_call x1, Pallas kernels, body(): pl.pallas_call(kernel, out_shape=(jax.ShapeDtypeStruct((1, 128, 1024), BF...  103 us

profile of v2, /device:TPU:15, one launch (start us, length us, event | category | flops | bytes accessed | tf_op | source)
XLA Modules:
  0.0 105.5 jit_solution(7482519981639288788)
XLA Ops:
  0.6 103.1 %value_path.1 = (bf16[1,128,1024]{2,1,0:T(8,128)(2,1)}, bf16[8,80,128]{2,1,0:T(8,128)(2,1)}) custom-call(bf16[1,128,5120]{2,1,0:T(8,128)(2,1)} %q_ref.1, bf16[1,128,1024]{2,1,0:T(8,128)(2,1)} %k_ref.1, bf16[1,128,5120]{2,1,0:T(8,128)(2,1)} %g_ref.1, bf16[1,128,5120]{2,1,0:T(8,128)(2,1)} %x_ref.1, s32[1,8,8]{2,1,0:T(8,128)} %mask_ref.1), custom_call_target="tpu_custom_call" | custom-call | tf_op jit(solution)/shard_map/value_path/pallas_call | solution.py:367
  103.7 1.7 %add_parts.1 = (bf16[1,128,1024]{2,1,0:T(8,128)(2,1)}, f32[80,128]{1,0:T(8,128)}) custom-call(bf16[1,128,1024]{2,1,0:T(8,128)(2,1)} %get-tuple-element.4.values_ref, bf16[8,80,128]{2,1,0:T(8,128)(2,1)} %get-tuple-element.5.parts_ref), custom_call_target="tpu_custom_call" | custom-call | tf_op jit(solution)/shard_map/add_parts/pallas_call | solution.py:406

commit v3 on v2

--- a/solution.py
+++ b/solution.py
@@ -16,13 +16,13 @@
 HIDDEN = -1e30
 X_AT = 8
 SHARE_AT = 8
-AHEAD = 3
+AHEAD = 5
 
 
 def kernel(
     q_ref, k_ref, g_ref, x_ref, mask_ref, vgrad_ref, parts_ref,
     qb, gb, kb, xin, xtl, xt, bias, vacc, vsend, vrecv, v2, ca, cb, ra, rb, sa, sb, fin,
-    own_sem, q_own, g_own, k_ss, k_rs, q_ss, q_rs, g_ss, g_rs, x_ss, x_rs, z_ss, z_rs, a_ss, a_rs,
+    ring_sem, z_sem, y_sem, core_sem, own_sem, q_own, g_own, k_ss, k_rs, q_ss, q_rs, g_ss, g_rs, x_ss, x_rs, z_ss, z_rs, a_ss, a_rs,
     f_ss, f_rs, ra_ss, ra_rs, rb_ss, rb_rs, fin_ss, fin_rs,
 ):
     d = lax.axis_index("dp")
@@ -88,34 +88,82 @@
     def greet(to):
         pl.semaphore_signal(barrier, inc=1, device_id=to, device_id_type=MESH)
 
-    for o in range(1, 8):
-        greet((d, lax.rem(t + o, 8)))
-    for o in range(4):
-        greet((d_core, lax.rem(x + o, 4) * 2 + zh))
-    for o in range(1, 8):
-        greet(place(x, lax.rem(y + o, 8), z, core))
-        if o != 4:
-            greet(place(x, y, lax.rem(z + o, 8), core))
-    for source in sources:
-        @pl.when(jnp.logical_not(mine(*source)))
-        def _():
-            greet(place(*source))
-    expected = 24
-    for to in dest:
-        expected = expected + jnp.where(mine(*to), 0, 1)
-    pl.semaphore_wait(barrier, expected)
+    def tell(sem, px):
+        pl.semaphore_signal(sem, inc=1, device_id=(d, px * 2 + zh), device_id_type=MESH)
+
+    @pl.when(x != 2)
+    def _():
+        greet((d, 4 + zh))
+
+    @pl.when(x == 2)
+    def _():
+        pl.semaphore_wait(barrier, 3)
+        for px in (0, 1, 3):
+            tell(ring_sem, px)
+
+    @pl.when(x != 2)
+    def _():
+        pl.semaphore_wait(ring_sem, 1)
+
+    def meet_z():
+        @pl.when(x == 0)
+        def _():
+            for o in range(1, 8):
+                greet(place(0, y, lax.rem(z + o, 8), core))
+            pl.semaphore_wait(barrier, 7)
+            for px in (1, 2, 3):
+                tell(z_sem, px)
+
+        @pl.when(x != 0)
+        def _():
+            pl.semaphore_wait(z_sem, 1)
+
+        @pl.when(x == 1)
+        def _():
+            for o in range(1, 8):
+                greet(place(1, lax.rem(y + o, 8), z, core))
+
+        @pl.when(x == 3)
+        def _():
+            greet((d_core, t))
+
+    def meet_rest():
+        @pl.when(x == 1)
+        def _():
+            pl.semaphore_wait(barrier, 7)
+            for px in (0, 2, 3):
+                tell(y_sem, px)
+
+        @pl.when(x == 3)
+        def _():
+            pl.semaphore_wait(barrier, 1)
+            for px in (0, 1, 2):
+                tell(core_sem, px)
+
+        @pl.when(x != 1)
+        def _():
+            pl.semaphore_wait(y_sem, 1)
+
+        @pl.when(x != 3)
+        def _():
+            pl.semaphore_wait(core_sem, 1)
 
     k_out = [[], []]
 
-    def send_keys(j):
-        for o in (4, 2, 6, 1, 7, 3, 5):
-            to = lax.rem(t + o, 8)
-            columns = pl.ds(pl.multiple_of(lax.div(to, 2) * 256 + j * 128, 128), 128)
-            k_out[j].append(send(
-                k_ref.at[0, :, columns], kb.at[j, t],
-                k_ss.at[j, o - 1], k_rs.at[j, o - 1], (d, to),
+    def send_keys(j, far):
+        new = []
+        for o in (0, 2, 1, 3) if far else (2, 1, 3):
+            tx = lax.rem(x + o, 4)
+            columns = pl.ds(pl.multiple_of(tx * 256 + j * 128, 128), 128)
+            i = o - 1 + 4 * far
+            new.append(send(
+                k_ref.at[0, :, columns], kb.at[j, t], k_ss.at[j, i], k_rs.at[j, i],
+                (d, tx * 2 + (1 - zh if far else zh)),
             ))
-        go(*k_out[j])
+        k_out[j].extend(new)
+        go(*new)
+        if far:
+            return
         columns = pl.ds(pl.multiple_of(x * 256 + j * 128, 128), 128)
         pltpu.make_async_copy(k_ref.at[0, :, columns], kb.at[j, t], own_sem.at[j, 0]).start()
 
@@ -140,9 +188,12 @@
         for copy in head_sends(h) + head_own(h):
             copy.start()
 
-    send_keys(0)
+    send_keys(0, False)
     pl.loop(0, AHEAD)(send_head)
-    send_keys(1)
+    send_keys(1, False)
+    meet_z()
+    send_keys(0, True)
+    send_keys(1, True)
 
     key_pos = lax.broadcasted_iota(jnp.int32, (128, 128), 0)
     query_pos = lax.broadcasted_iota(jnp.int32, (128, 128), 1)
@@ -231,6 +282,10 @@
                 send_head(h + AHEAD)
 
             if j == 1:
+                @pl.when(h == GROUP)
+                def _():
+                    meet_rest()
+
                 @pl.when(h == SHARE_AT)
                 def _():
                     share(0)
@@ -363,7 +418,7 @@
 
 
 def body(query_states, key_states, out_grad, layer_input, block_mask):
-    vmem, dma = pltpu.VMEM, pltpu.SemaphoreType.DMA
+    vmem, dma, regular = pltpu.VMEM, pltpu.SemaphoreType.DMA, pltpu.SemaphoreType.REGULAR
     values, parts = pl.pallas_call(
         kernel,
         out_shape=(
@@ -391,6 +446,7 @@
             vmem((2, 2, 80, 128), BF16),
             vmem((2, 2, 80, 128), BF16),
             vmem((8, 80, 128), BF16),
+            regular, regular, regular, regular,
             dma((2, 4)),
             dma((10,)), dma((10,)),
             dma((2, 7)), dma((2, 7)), dma((10, 3)), dma((10, 3)), dma((10, 3)), dma((10, 3)),

time: 106 us -> 105 us (level)
  the two profiles are of different devices: /device:TPU:15 before, /device:TPU:265 now
where the time goes in v3:
time: 105 us; the launch traced here: 104 us
  Pallas kernels  104 us (99%)
    pallas_call x1, Pallas kernels, body(): pl.pallas_call(kernel, out_shape=(jax.ShapeDtypeStruct((1, 128, 1024), BF...  102 us

profile of v3, /device:TPU:265, one launch (start us, length us, event | category | flops | bytes accessed | tf_op | source)
XLA Modules:
  0.0 104.4 jit_solution(6861698235881967080)
XLA Ops:
  0.6 102.1 %value_path.1 = (bf16[1,128,1024]{2,1,0:T(8,128)(2,1)}, bf16[8,80,128]{2,1,0:T(8,128)(2,1)}) custom-call(bf16[1,128,5120]{2,1,0:T(8,128)(2,1)} %q_ref.1, bf16[1,128,1024]{2,1,0:T(8,128)(2,1)} %k_ref.1, bf16[1,128,5120]{2,1,0:T(8,128)(2,1)} %g_ref.1, bf16[1,128,5120]{2,1,0:T(8,128)(2,1)} %x_ref.1, s32[1,8,8]{2,1,0:T(8,128)} %mask_ref.1), custom_call_target="tpu_custom_call" | custom-call | tf_op jit(solution)/shard_map/value_path/pallas_call | solution.py:422
  102.7 1.7 %add_parts.1 = (bf16[1,128,1024]{2,1,0:T(8,128)(2,1)}, f32[80,128]{1,0:T(8,128)}) custom-call(bf16[1,128,1024]{2,1,0:T(8,128)(2,1)} %get-tuple-element.4.values_ref, bf16[8,80,128]{2,1,0:T(8,128)(2,1)} %get-tuple-element.5.parts_ref), custom_call_target="tpu_custom_call" | custom-call | tf_op jit(solution)/shard_map/add_parts/pallas_call | solution.py:462

commit v4 on v3

--- a/solution.py
+++ b/solution.py
@@ -14,7 +14,7 @@
 F32 = jnp.float32
 MESH = pl.DeviceIdType.MESH
 HIDDEN = -1e30
-X_AT = 8
+X_AT = 9
 SHARE_AT = 8
 AHEAD = 5
 
@@ -148,24 +148,29 @@
         def _():
             pl.semaphore_wait(core_sem, 1)
 
-    k_out = [[], []]
-
-    def send_keys(j, far):
-        new = []
-        for o in (0, 2, 1, 3) if far else (2, 1, 3):
+    k_out, k_far = [[], []], []
+
+    def own_keys(j):
+        columns = pl.ds(pl.multiple_of(x * 256 + j * 128, 128), 128)
+        return pltpu.make_async_copy(k_ref.at[0, :, columns], kb.at[j, zh, x], own_sem.at[j, 0])
+
+    def send_keys(j):
+        for o in (2, 1, 3):
             tx = lax.rem(x + o, 4)
             columns = pl.ds(pl.multiple_of(tx * 256 + j * 128, 128), 128)
-            i = o - 1 + 4 * far
-            new.append(send(
-                k_ref.at[0, :, columns], kb.at[j, t], k_ss.at[j, i], k_rs.at[j, i],
-                (d, tx * 2 + (1 - zh if far else zh)),
+            k_out[j].append(send(
+                k_ref.at[0, :, columns], kb.at[j, zh, x], k_ss.at[j, o], k_rs.at[j, o],
+                (d, tx * 2 + zh),
             ))
-        k_out[j].extend(new)
-        go(*new)
-        if far:
-            return
-        columns = pl.ds(pl.multiple_of(x * 256 + j * 128, 128), 128)
-        pltpu.make_async_copy(k_ref.at[0, :, columns], kb.at[j, t], own_sem.at[j, 0]).start()
+        go(*k_out[j])
+        own_keys(j).start()
+
+    def send_half(j):
+        arrive(*k_out[j])
+        own_keys(j).wait()
+        half = kb.at[j, zh]
+        k_far.append(send(half, half, k_ss.at[j, 0], k_rs.at[j, 0], (d, x * 2 + 1 - zh)))
+        go(k_far[j])
 
     def head_sends(h):
         out = []
@@ -188,12 +193,12 @@
         for copy in head_sends(h) + head_own(h):
             copy.start()
 
-    send_keys(0, False)
+    send_keys(0)
+    send_keys(1)
     pl.loop(0, AHEAD)(send_head)
-    send_keys(1, False)
     meet_z()
-    send_keys(0, True)
-    send_keys(1, True)
+    send_half(0)
+    send_half(1)
 
     key_pos = lax.broadcasted_iota(jnp.int32, (128, 128), 0)
     query_pos = lax.broadcasted_iota(jnp.int32, (128, 128), 1)
@@ -209,7 +214,7 @@
     def attend(j, h):
         for k in range(4):
             n = (2 * k + 2) * 128
-            keys = kb[j, 0 : 2 * k + 2].reshape(n, 128)
+            keys = jnp.concatenate([kb[j, c % 2, c // 2] for c in range(2 * k + 2)], axis=0)
             s = lax.dot_general(
                 keys, qb[h, k], (((1,), (1,)), ((), ())), preferred_element_type=F32
             )
@@ -267,8 +272,7 @@
             copy.start()
 
     for j in range(2):
-        arrive(*k_out[j])
-        pltpu.make_async_copy(k_ref.at[0, :, 0:128], kb.at[j, t], own_sem.at[j, 0]).wait()
+        arrive(k_far[j])
 
         @pl.loop(j * GROUP, (j + 1) * GROUP)
         def _(h):
@@ -344,36 +348,35 @@
                 cb.at[j, tz], rb.at[j, z], rb_ss.at[j, o - 1], rb_rs.at[j, o - 1],
                 place(x, y, tz, core),
             ))
-            go(ra_out[j][-1], rb_out[j][-1])
+        go(*rb_out[j])
+        go(*ra_out[j])
 
     fin_out = []
 
-    def second_sum(j):
-        arrive(*ra_out[j], *rb_out[j])
-        for own_part, parts, me, out in ((ca, ra, y, sa), (cb, rb, z, sb)):
-            for m in range(2):
-                total = own_part[j, me, m].astype(F32)
-                for o in range(1, 8):
-                    total += parts[j, lax.rem(me + o, 8), m].astype(F32)
-                out[j, m] = total.astype(BF16)
-        for i in range(4):
-            src = (sa if i < 2 else sb).at[j, i % 2]
-            slot = z if i < 2 else y
-            to = dest[j * 4 + i]
-            copy = send(src, fin.at[slot], fin_ss.at[j * 4 + i], fin_rs.at[slot], place(*to))
+    def second_sum(j, by_z):
+        arrive(*(rb_out if by_z else ra_out)[j])
+        own_part, parts, me, out, slot = (cb, rb, z, sb, y) if by_z else (ca, ra, y, sa, z)
+        for m in range(2):
+            total = own_part[j, me, m].astype(F32)
+            for o in range(1, 8):
+                total += parts[j, lax.rem(me + o, 8), m].astype(F32)
+            out[j, m] = total.astype(BF16)
+            i = j * 4 + 2 * by_z + m
+            to = dest[i]
+            copy = send(out.at[j, m], fin.at[slot], fin_ss.at[i], fin_rs.at[slot], place(*to))
             fin_out.append((copy, to))
             here = mine(*to)
 
             @pl.when(here)
             def _():
-                fin[slot] = src[...]
+                fin[slot] = out[j, m]
 
             @pl.when(jnp.logical_not(here))
             def _():
                 copy.start()
 
+    share(1)
     forward(0)
-    share(1)
     for copy in x_out:
         copy.wait_recv()
     own_x.wait()
@@ -384,8 +387,9 @@
         vgrad_ref[0, :, g * 128 : (g + 1) * 128] = v2[core, g, pl.ds(pl.multiple_of(x * 128, 128), 128)]
     multiply(1)
     first_sum(1)
-    second_sum(0)
-    second_sum(1)
+    for j in range(2):
+        second_sum(j, True)
+        second_sum(j, False)
 
     for s, source in enumerate(sources):
         @pl.when(jnp.logical_not(mine(*source)))
@@ -430,7 +434,7 @@
         scratch_shapes=[
             vmem((10, 4, 128, 128), BF16),
             vmem((10, 4, 128, 128), BF16),
-            vmem((2, 8, 128, 128), BF16),
+            vmem((2, 2, 4, 128, 128), BF16),
             vmem((128, 5120), BF16),
             vmem((8, 640, 128), BF16),
             vmem((640, 1024), BF16),
@@ -449,7 +453,7 @@
             regular, regular, regular, regular,
             dma((2, 4)),
             dma((10,)), dma((10,)),
-            dma((2, 7)), dma((2, 7)), dma((10, 3)), dma((10, 3)), dma((10, 3)), dma((10, 3)),
+            dma((2, 4)), dma((2, 4)), dma((10, 3)), dma((10, 3)), dma((10, 3)), dma((10, 3)),
             dma((7,)), dma((7,)), dma((2,)), dma((2,)), dma((2, 4)), dma((2, 4)),
             dma((2, 4)), dma((2, 4)), dma((2, 7)), dma((2, 7)), dma((2, 7)), dma((2, 7)),
             dma((8,)), dma((8,)),

time: 105 us -> 101 us (0.962)
  Pallas kernels: 104 us -> 100 us
    pallas_call x1, Pallas kernels: 102 us -> 98.7 us  [body(): pl.pallas_call(kernel, out_shape=(jax.ShapeDtypeStruct((1, 128, 1024), BF...]
where the time goes in v4:
time: 101 us
  Pallas kernels  100 us (99%)
    pallas_call x1, Pallas kernels, body(): pl.pallas_call(kernel, out_shape=(jax.ShapeDtypeStruct((1, 128, 1024), BF...  98.7 us

profile of v4, /device:TPU:265, one launch (start us, length us, event | category | flops | bytes accessed | tf_op | source)
XLA Modules:
  0.0 101.1 jit_solution(5074487607947653026)
XLA Ops:
  0.6 98.7 %value_path.1 = (bf16[1,128,1024]{2,1,0:T(8,128)(2,1)}, bf16[8,80,128]{2,1,0:T(8,128)(2,1)}) custom-call(bf16[1,128,5120]{2,1,0:T(8,128)(2,1)} %q_ref.1, bf16[1,128,1024]{2,1,0:T(8,128)(2,1)} %k_ref.1, bf16[1,128,5120]{2,1,0:T(8,128)(2,1)} %g_ref.1, bf16[1,128,5120]{2,1,0:T(8,128)(2,1)} %x_ref.1, s32[1,8,8]{2,1,0:T(8,128)} %mask_ref.1), custom_call_target="tpu_custom_call" | custom-call | tf_op jit(solution)/shard_map/value_path/pallas_call | solution.py:426
  99.4 1.7 %add_parts.1 = (bf16[1,128,1024]{2,1,0:T(8,128)(2,1)}, f32[80,128]{1,0:T(8,128)}) custom-call(bf16[1,128,1024]{2,1,0:T(8,128)(2,1)} %get-tuple-element.4.values_ref, bf16[8,80,128]{2,1,0:T(8,128)(2,1)} %get-tuple-element.5.parts_ref), custom_call_target="tpu_custom_call" | custom-call | tf_op jit(solution)/shard_map/add_parts/pallas_call | solution.py:466

commit v5 on v4

--- a/solution.py
+++ b/solution.py
@@ -256,11 +256,14 @@
     a_out, f_out = [[], []], [[], []]
     for j in range(2):
         mine_v = v2.at[core, 2 * x + j]
-        for o in (2, 1, 3):
-            a_out[j].append(send(
-                mine_v, mine_v, a_ss.at[j, o], a_rs.at[j, o], (d, lax.rem(x + o, 4) * 2 + zh)
-            ))
-        f_out[j].append(send(mine_v, mine_v, f_ss.at[j, 0], f_rs.at[j, 0], (d_core, t)))
+        for part in range(2):
+            some = mine_v.at[pl.ds(part * 256, 256)]
+            for o in (2, 1, 3):
+                a_out[j].append(send(
+                    some, some, a_ss.at[j, part, o], a_rs.at[j, part, o],
+                    (d, lax.rem(x + o, 4) * 2 + zh),
+                ))
+        f_out[j].append(send(mine_v, mine_v, f_ss.at[j, 0, 0], f_rs.at[j, 0, 0], (d_core, t)))
 
     def share(j):
         z_out[j].wait_recv()
@@ -306,10 +309,13 @@
         z_out[j].start()
 
     def forward(j):
-        for o, copy in zip((2, 1, 3), a_out[j]):
+        for i, copy in enumerate(a_out[j]):
+            part, o = i // 3, (2, 1, 3)[i % 3]
             copy.wait_recv()
-            block = v2.at[core, 2 * lax.rem(x + 4 - o, 4) + j]
-            f_out[j].append(send(block, block, f_ss.at[j, o], f_rs.at[j, o], (d_core, t)))
+            block = v2.at[core, 2 * lax.rem(x + 4 - o, 4) + j, pl.ds(part * 256, 256)]
+            f_out[j].append(send(
+                block, block, f_ss.at[j, part, o], f_rs.at[j, part, o], (d_core, t)
+            ))
             f_out[j][-1].start()
 
     def multiply(j):
@@ -454,8 +460,8 @@
             dma((2, 4)),
             dma((10,)), dma((10,)),
             dma((2, 4)), dma((2, 4)), dma((10, 3)), dma((10, 3)), dma((10, 3)), dma((10, 3)),
-            dma((7,)), dma((7,)), dma((2,)), dma((2,)), dma((2, 4)), dma((2, 4)),
-            dma((2, 4)), dma((2, 4)), dma((2, 7)), dma((2, 7)), dma((2, 7)), dma((2, 7)),
+            dma((7,)), dma((7,)), dma((2,)), dma((2,)), dma((2, 2, 4)), dma((2, 2, 4)),
+            dma((2, 2, 4)), dma((2, 2, 4)), dma((2, 7)), dma((2, 7)), dma((2, 7)), dma((2, 7)),
             dma((8,)), dma((8,)),
         ],
         compiler_params=pltpu.CompilerParams(

time: 101 us -> 101 us (level)
  no operation moved by 1% of the time
where the time goes in v5:
time: 101 us
  Pallas kernels  100 us (99%)
    pallas_call x1, Pallas kernels, body(): pl.pallas_call(kernel, out_shape=(jax.ShapeDtypeStruct((1, 128, 1024), BF...  98.7 us

profile of v5, /device:TPU:265, one launch (start us, length us, event | category | flops | bytes accessed | tf_op | source)
XLA Modules:
  0.0 101.0 jit_solution(9569306779018452615)
XLA Ops:
  0.6 98.7 %value_path.1 = (bf16[1,128,1024]{2,1,0:T(8,128)(2,1)}, bf16[8,80,128]{2,1,0:T(8,128)(2,1)}) custom-call(bf16[1,128,5120]{2,1,0:T(8,128)(2,1)} %q_ref.1, bf16[1,128,1024]{2,1,0:T(8,128)(2,1)} %k_ref.1, bf16[1,128,5120]{2,1,0:T(8,128)(2,1)} %g_ref.1, bf16[1,128,5120]{2,1,0:T(8,128)(2,1)} %x_ref.1, s32[1,8,8]{2,1,0:T(8,128)} %mask_ref.1), custom_call_target="tpu_custom_call" | custom-call | tf_op jit(solution)/shard_map/value_path/pallas_call | solution.py:432
  99.3 1.7 %add_parts.1 = (bf16[1,128,1024]{2,1,0:T(8,128)(2,1)}, f32[80,128]{1,0:T(8,128)}) custom-call(bf16[1,128,1024]{2,1,0:T(8,128)(2,1)} %get-tuple-element.4.values_ref, bf16[8,80,128]{2,1,0:T(8,128)(2,1)} %get-tuple-element.5.parts_ref), custom_call_target="tpu_custom_call" | custom-call | tf_op jit(solution)/shard_map/add_parts/pallas_call | solution.py:472
